TPU v7x, 512 devices: a whole 4x8x8 slice. The times are simulated.
512 devices in a mesh: tm: 128 (over z_lo, x, y, core), rows: 4 (over z_hi).
Axes of the slice: x: 4, y: 8, z: 8 (z_hi: 4, z_lo: 2; z = z_hi * 2 + z_lo), core: 2. Of those that a mesh axis runs over, the one named last changes fastest.
Arguments:
- coupling: float32 [128, 1024, 1024], P('tm', 'rows'), may hold values from -0.078125 to 0.078125
- field: float32 [128, 1024], P('tm', 'rows'), may hold values from -1.2 to 1.2
Outputs:
- reduced: float32 [128, 1024, 1024], P('tm', 'rows')
All inputs are finite; a program needn't handle non-finite values.
Results may differ from a plain program's by a relative error of at most 0.00015.
Values sent between devices are 32-bit elements; how exact they have to be, the bound alone decides.
A program may use at most 64 MiB of HBM per device.

v0:
```python
import jax
import jax.numpy as jnp
from jax import lax
from jax.sharding import PartitionSpec as P


def shifted(x, axis, by):
    count = lax.axis_size(axis)
    return lax.ppermute(x, axis, [(i, (i + by) % count) for i in range(count)])


def per_device(coupling, field):
    nrow = coupling.shape[1]
    nsite = coupling.shape[2]
    first = lax.axis_index("rows") * nrow
    row_ids = lax.broadcasted_iota(jnp.int32, (nrow, nsite), 0) + first
    col_ids = lax.broadcasted_iota(jnp.int32, (nrow, nsite), 1)
    ident = jnp.where(row_ids == col_ids, 1.0, 0.0).astype(jnp.float32)
    mine = jnp.exp(field[0])[:, None] * (ident + coupling[0])
    whole_own = lax.all_gather(mine, "rows", axis=0, tiled=True)
    whole_next = shifted(whole_own, "tm", -1)
    paired_full = jnp.matmul(whole_next, whole_own, precision=lax.Precision.HIGHEST)
    paired_rows = lax.dynamic_slice_in_dim(paired_full, first, nrow, 0)
    ahead = shifted(paired_rows, "tm", -2)
    result = jnp.matmul(ahead, paired_full, precision=lax.Precision.HIGHEST)
    return result[None]


def solution(mesh):
    in_specs = (P("tm", "rows", None), P("tm", "rows"))
    out_specs = P("tm", "rows", None)
    return jax.shard_map(
        per_device, mesh=mesh, in_specs=in_specs, out_specs=out_specs, check_vma=False
    )
```

profile of v0, /device:TPU:1, one launch (start us, length us, event | category | flops | bytes accessed | tf_op | source)
XLA Modules:
  0.0 214.2 jit_solution(8705998858939211881)
XLA Ops:
  6.5 0.0 all-gather.2.cloned.1.call-start
  6.5 0.7 exp.10
  7.2 2.5 %fusion = f32[256,1024]{1,0:T(8,128)} fusion(f32[1,256,1024]{2,1,0:T(8,128)} %param.2, s32[256]{0:T(256)S(1)} %iota_add_fusion, f32[256]{0:T(256)S(1)} %bitcast.11), kind=kLoop, calls=%fused_computation.2 | loop fusion | flops 1048576 | bytes 2099200 | tf_op jit(solution)/shard_map/mul | solution.py:19
  9.7 0.0 all-gather.2.cloned.1.call-update
  9.8 95.2 %all-gather.2.cloned.1.call-done = f32[1024,1024]{1,0:T(8,128)} async-done(((f32[256,1024]{1,0:T(8,128)}), f32[1024,1024]{1,0:T(8,128)}) %all-gather.2.cloned.1.call-update) | async-done | bytes 4194320 | tf_op jit(solution)/shard_map/all_gather | solution.py:20
  104.9 2.6 %collective-permute-start = (f32[1024,1024]{1,0:T(8,128)}, f32[1024,1024]{1,0:T(8,128)}, u32[]{:S(2)}, u32[]{:S(2)}) collective-permute-start(f32[1024,1024]{1,0:T(8,128)} %all-gather.2.cloned.1.call-done), channel_id=1, source_target_pairs={{0,508},{4,0},{8,4},{12,8},{16,12},{20,16},{24,20},{28,24},{32,28}... | collective-permute-start | bytes 12582920 | tf_op jit(solution)/shard_map/ppermute | solution.py:9
  107.5 47.5 %collective-permute-done = f32[1024,1024]{1,0:T(8,128)} collective-permute-done((f32[1024,1024]{1,0:T(8,128)}, f32[1024,1024]{1,0:T(8,128)}, u32[]{:S(2)}, u32[]{:S(2)}) %collective-permute-start) | collective-permute-done | bytes 4194336 | tf_op jit(solution)/shard_map/ppermute | solution.py:9
  155.1 16.9 %fusion.1 = f32[1024,1024]{1,0:T(8,128)S(1)} fusion(f32[1024,1024]{1,0:T(8,128)} %collective-permute-done, f32[1024,1024]{1,0:T(8,128)} %all-gather.2.cloned.1.call-done), kind=kOutput, calls=%fused_computation.6 | convolution fusion | flops 12884901888 | bytes 12582912 | tf_op jit(solution)/shard_map/dot_general | solution.py:22
  171.9 0.1 constant_dynamic-slice_fusion
  172.1 11.8 %collective-permute-start.1 = (f32[256,1024]{1,0:T(8,128)S(1)}, f32[256,1024]{1,0:T(8,128)S(1)}, u32[]{:S(2)}, u32[]{:S(2)}) collective-permute-start(f32[256,1024]{1,0:T(8,128)S(1)} %constant_dynamic-slice_fusion), channel_id=1, source_target_pairs={{0,504},{4,508},{8,0},{12,4},{16,8},{20,12},{24,16},{28,20},{32,24... | collective-permute-start | bytes 3145736 | tf_op jit(solution)/shard_map/ppermute | solution.py:9
  183.9 18.8 %collective-permute-done.1 = f32[256,1024]{1,0:T(8,128)S(1)} collective-permute-done((f32[256,1024]{1,0:T(8,128)S(1)}, f32[256,1024]{1,0:T(8,128)S(1)}, u32[]{:S(2)}, u32[]{:S(2)}) %collective-permute-start.1) | collective-permute-done | bytes 1048608 | tf_op jit(solution)/shard_map/ppermute | solution.py:9
  202.7 4.7 %convolution_bitcast_fusion = f32[1,256,1024]{2,1,0:T(8,128)} fusion(f32[256,1024]{1,0:T(8,128)S(1)} %collective-permute-done.1, f32[1024,1024]{1,0:T(8,128)S(1)} %fusion.1), kind=kOutput, calls=%fused_computation | convolution fusion | flops 3221225472 | bytes 6291456 | tf_op jit(solution)/shard_map/dot_general | solution.py:25
  (1 shorter events, 0.0 us)
Async XLA Ops:
  6.5 98.4 %all-gather.2.cloned.1.call-start = ((), (), s32[]{:S(2)}) async-start(), calls=%async_computation | async-start | bytes 5242880 | tf_op jit(solution)/shard_map/all_gather | solution.py:20
  104.9 50.1 %collective-permute-start = (f32[1024,1024]{1,0:T(8,128)}, f32[1024,1024]{1,0:T(8,128)}, u32[]{:S(2)}, u32[]{:S(2)}) collective-permute-start(f32[1024,1024]{1,0:T(8,128)} %all-gather.2.cloned.1.call-done), channel_id=1, source_target_pairs={{0,508},{4,0},{8,4},{12,8},{16,12},{20,16},{24,20},{28,24},{32,28}... | collective-permute-start | bytes 12582920 | tf_op jit(solution)/shard_map/ppermute | solution.py:9
  172.1 30.7 %collective-permute-start.1 = (f32[256,1024]{1,0:T(8,128)S(1)}, f32[256,1024]{1,0:T(8,128)S(1)}, u32[]{:S(2)}, u32[]{:S(2)}) collective-permute-start(f32[256,1024]{1,0:T(8,128)S(1)} %constant_dynamic-slice_fusion), channel_id=1, source_target_pairs={{0,504},{4,508},{8,0},{12,4},{16,8},{20,12},{24,16},{28,20},{32,24... | collective-permute-start | bytes 3145736 | tf_op jit(solution)/shard_map/ppermute | solution.py:9
Sparse Core Ops, SparseCore 0:
  9.9 94.9 all-gather.1
where the time goes:
time: 214 us
  waiting for transfers between devices  162 us (76%)
  matrix products  21.5 us (10%)
  starting transfers between devices  14.4 us (7%)
  between operations  13.4 us (6%)
  other arithmetic  2.51 us (1%)
    all_gather x1, waiting for transfers between devices, per_device(): whole_own = lax.all_gather(mine, 'rows', axis=0, tiled=True)  95.2 us
    ppermute x2, waiting for transfers between devices, shifted(): return lax.ppermute(x, axis, [(i, (i + by) % count) for i in range(count)])  66.4 us
    dot_general x1, matrix products, per_device(): jnp.matmul(whole_next, whole_own, precision=lax.Precision.HIGHEST)  16.9 us
    ppermute x2, starting transfers between devices, shifted(): return lax.ppermute(x, axis, [(i, (i + by) % count) for i in range(count)])  14.4 us
    dot_general x1, matrix products, per_device(): result = jnp.matmul(ahead, paired_full, precision=lax.Precision.HIGHEST)  4.67 us
  transfers between devices with their start and end apart: 3, of which 3 were waited for; matrix products, arithmetic and copies ran while one was open for 0% of the time, Pallas kernels for 0%

commit v1 on v0

v1 whole, which is shorter than its diff:
```python
import functools

import jax
import jax.numpy as jnp
from jax import lax
from jax.experimental import pallas as pl
from jax.experimental.pallas import tpu as pltpu
from jax.sharding import PartitionSpec as P

F32 = jnp.float32
BF16 = jnp.bfloat16
MESH = pl.DeviceIdType.MESH

WIDE = 128
AHEAD = 2
START = 6


def split(x):
    hi = x.astype(BF16)
    return hi, (x - hi.astype(F32)).astype(BF16)


def dot3(ah, al, bh, bl):
    def mm(a, b):
        return jnp.dot(a, b, preferred_element_type=F32)

    return mm(ah, bh) + (mm(ah, bl) + mm(al, bh))


def kernel(
    n_t, n_r, coupling, field, out,
    raw, full, sib, rowbuf, lhs_h, lhs_l, own_h, own_l, one_h, one_l,
    stage_a, stage_b, land_a, land_b, acc, res,
    local_sem, out_sem,
    own_s, own_r, fwd_s, fwd_r, sib_s, sib_r, xo_s, xo_r, row_s, row_r, a_s, a_r, b_s, b_r,
):
    t = lax.axis_index("tm")
    r = lax.axis_index("rows")
    rows = raw.shape[0]
    nch = full.shape[0]
    even = lax.rem(t, 2) == 0
    half = rows // 2

    def tm(by):
        return lax.rem(t + by + n_t, n_t)

    def at_t(by):
        return (tm(by), r)

    def at_r(by):
        return (t, lax.rem(r + by + n_r, n_r))

    def plane(by):
        return pl.multiple_of(lax.rem(r + by + n_r, n_r) * rows, rows)

    load = pltpu.make_async_copy(coupling.at[0], raw, local_sem)
    load.start()

    barrier = pltpu.get_barrier_semaphore()
    for by in (1, -1):
        pl.semaphore_signal(barrier, inc=1, device_id=at_r(by), device_id_type=MESH)
    pl.semaphore_signal(barrier, inc=1, device_id=at_t(1), device_id_type=MESH)

    @pl.when(even)
    def _():
        pl.semaphore_signal(barrier, inc=1, device_id=at_t(2), device_id_type=MESH)

    def copy(src, dst, ssem, rsem, dev):
        return pltpu.make_async_remote_copy(
            src_ref=src, dst_ref=dst, send_sem=ssem, recv_sem=rsem,
            device_id=dev, device_id_type=MESH,
        )

    def own(c, d):
        piece = full.at[c, pl.ds(plane(0), rows), :]
        return copy(piece, piece, own_s.at[d, c], own_r.at[d, c], at_r(1 - 2 * d))

    def own_in(c, d):
        piece = full.at[c, pl.ds(plane(2 * d - 1), rows), :]
        return copy(piece, piece, own_s.at[d, c], own_r.at[d, c], at_r(1 - 2 * d))

    def fwd(c, d):
        piece = full.at[c, pl.ds(pl.multiple_of(plane(2 * d - 1) + d * half, half), half), :]
        return copy(piece, piece, fwd_s.at[d, c], fwd_r.at[d, c], at_r(1 - 2 * d))

    def fwd_in(c, d):
        piece = full.at[c, pl.ds(pl.multiple_of(plane(2) + d * half, half), half), :]
        return copy(piece, piece, fwd_s.at[d, c], fwd_r.at[d, c], at_r(1 - 2 * d))

    def to_sib(c):
        return copy(full.at[c], sib.at[c], sib_s.at[c], sib_r.at[c], at_t(-1))

    def xo(c):
        return copy(stage_a.at[c], land_a.at[c], xo_s.at[c], xo_r.at[c], at_t(-1))

    def row():
        return copy(full.at[:, pl.ds(plane(0), rows), :], rowbuf, row_s, row_r, at_t(-1))

    def send_a(c):
        return copy(stage_a.at[c], land_b.at[c], a_s.at[c], a_r.at[c], at_t(-2))

    def send_b(c):
        return copy(stage_b.at[c], land_b.at[c], b_s.at[c], b_r.at[c], at_t(-1))

    def cols(c):
        return pl.ds(pl.multiple_of(c * WIDE, WIDE), WIDE)

    scale = jnp.exp(jnp.transpose(jnp.broadcast_to(field[...], (WIDE, rows))))
    load.wait()
    row_ids = lax.broadcasted_iota(jnp.int32, (rows, WIDE), 0) + r * rows
    col_ids = lax.broadcasted_iota(jnp.int32, (rows, WIDE), 1)

    def build(c, _):
        ident = jnp.where(row_ids == col_ids + c * WIDE, 1.0, 0.0).astype(F32)
        full[c, pl.ds(plane(0), rows), :] = scale * (ident + raw[:, cols(c)])
        return 0

    lax.fori_loop(0, nch, build, 0)

    def gather(process):
        for c in range(AHEAD):
            for d in (0, 1):
                own(c, d).start()

        def step(c, _):
            @pl.when(c < nch)
            def _():
                for d in (0, 1):
                    own_in(c, d).wait_recv()
                    fwd(c, d).start()

            @pl.when(c + AHEAD < nch)
            def _():
                for d in (0, 1):
                    own(c + AHEAD, d).start()

            @pl.when(c >= 1)
            def _():
                for d in (0, 1):
                    fwd_in(c - 1, d).wait_recv()
                process(c - 1)

            return 0

        lax.fori_loop(0, nch + 1, step, 0)

    def drain(c, _):
        for d in (0, 1):
            own(c, d).wait_send()
            fwd(c, d).wait_send()
        return 0

    def fill_lhs(c, first):
        hi, lo = split(rowbuf[c])
        lhs_h[first : first + rows, cols(c)] = hi
        lhs_l[first : first + rows, cols(c)] = lo

    def add_chunk(c, land, total):
        h, l = split(land[c])
        total[...] += dot3(h, l, one_h[cols(c), :], one_l[cols(c), :])

    @pl.when(jnp.logical_not(even))
    def _():
        pl.semaphore_wait(barrier, 3)
        row().start()

        def left_factor():
            row().wait_recv()

            def body(c, _):
                fill_lhs(c, 0)
                return 0

            lax.fori_loop(0, nch, body, 0)

        def product(c):
            stage_a[c] = dot3(
                lhs_h[0:rows, :], lhs_l[0:rows, :], one_h[:, cols(c)], one_l[:, cols(c)]
            )
            xo(c).start()

        lag = 3

        def process(c):
            to_sib(c).start()
            hi, lo = split(full[c])
            one_h[:, cols(c)] = hi
            one_l[:, cols(c)] = lo

            @pl.when(c == lag)
            def _():
                left_factor()

            @pl.when(c >= lag)
            def _():
                product(c - lag)

        gather(process)

        def rest(c, _):
            product(c)
            return 0

        lax.fori_loop(nch - lag, nch, rest, 0)

        acc[...] = jnp.zeros_like(acc)

        def body(c, _):
            send_b(c).wait_recv()
            add_chunk(c, land_b, acc)
            return 0

        lax.fori_loop(0, nch, body, 0)
        write = pltpu.make_async_copy(acc, out.at[0], out_sem.at[0])
        write.start()
        row().wait_send()

        def finish(c, _):
            to_sib(c).wait_send()
            xo(c).wait_send()
            return 0

        lax.fori_loop(0, nch, finish, 0)
        lax.fori_loop(0, nch, drain, 0)
        write.wait()

    @pl.when(even)
    def _():
        pl.semaphore_wait(barrier, 4)
        row().start()
        row().wait_recv()

        def fill(c, _):
            fill_lhs(c, 0)
            return 0

        lax.fori_loop(0, nch, fill, 0)

        def take(c, _):
            to_sib(c).wait_recv()
            hi, lo = split(sib[c])
            one_h[:, cols(c)] = hi
            one_l[:, cols(c)] = lo
            return 0

        lax.fori_loop(0, START, take, 0)
        acc[...] = jnp.zeros_like(acc)
        lag = 2

        def process(c):
            @pl.when(c == 0)
            def _():
                lax.fori_loop(START, nch, take, 0)

                def body(k, _):
                    xo(k).wait_recv()
                    hi, lo = split(land_a[k])
                    lhs_h[rows : 2 * rows, cols(k)] = hi
                    lhs_l[rows : 2 * rows, cols(k)] = lo
                    return 0

                lax.fori_loop(0, nch, body, 0)

            bh, bl = split(full[c])
            own_h[:, cols(c)] = bh
            own_l[:, cols(c)] = bl
            y = dot3(lhs_h[...], lhs_l[...], bh, bl)
            stage_a[c] = y[0:rows]
            send_a(c).start()
            stage_b[c] = y[rows:]
            send_b(c).start()

            @pl.when(c >= lag)
            def _():
                send_a(c - lag).wait_recv()
                add_chunk(c - lag, land_b, acc)

        gather(process)

        def rest(c, _):
            send_a(c).wait_recv()
            add_chunk(c, land_b, acc)
            return 0

        lax.fori_loop(nch - lag, nch, rest, 0)

        xh, xl = split(acc[...])
        wide = 2 * WIDE
        for k in range(nch // 2):
            part = slice(k * wide, (k + 1) * wide)
            res[k] = dot3(xh, xl, own_h[:, part], own_l[:, part])
            pltpu.make_async_copy(res.at[k], out.at[0, :, part], out_sem.at[k]).start()
        row().wait_send()

        def finish(c, _):
            send_a(c).wait_send()
            send_b(c).wait_send()
            return 0

        lax.fori_loop(0, nch, finish, 0)
        lax.fori_loop(0, nch, drain, 0)
        for k in range(nch // 2):
            part = slice(k * wide, (k + 1) * wide)
            pltpu.make_async_copy(res.at[k], out.at[0, :, part], out_sem.at[k]).wait()


def per_device(n_t, n_r, coupling, field):
    _, rows, sites = coupling.shape
    nch = sites // WIDE
    dma = pltpu.SemaphoreType.DMA
    piece = pltpu.VMEM((nch, rows, WIDE), F32)
    whole = pltpu.VMEM((nch, sites, WIDE), F32)
    return pl.pallas_call(
        functools.partial(kernel, n_t, n_r),
        out_shape=jax.ShapeDtypeStruct((1, rows, sites), F32),
        in_specs=[
            pl.BlockSpec(memory_space=pl.ANY),
            pl.BlockSpec(memory_space=pltpu.VMEM),
        ],
        out_specs=pl.BlockSpec(memory_space=pl.ANY),
        scratch_shapes=[
            pltpu.VMEM((rows, sites), F32),
            whole,
            whole,
            piece,
            pltpu.VMEM((2 * rows, sites), BF16),
            pltpu.VMEM((2 * rows, sites), BF16),
            pltpu.VMEM((sites, sites), BF16),
            pltpu.VMEM((sites, sites), BF16),
            pltpu.VMEM((sites, sites), BF16),
            pltpu.VMEM((sites, sites), BF16),
            piece,
            piece,
            piece,
            piece,
            pltpu.VMEM((rows, sites), F32),
            pltpu.VMEM((nch // 2, rows, 2 * WIDE), F32),
            dma,
            dma((nch,)),
            dma((2, nch)),
            dma((2, nch)),
            dma((2, nch)),
            dma((2, nch)),
            dma((nch,)),
            dma((nch,)),
            dma((nch,)),
            dma((nch,)),
            dma,
            dma,
            dma((nch,)),
            dma((nch,)),
            dma((nch,)),
            dma((nch,)),
        ],
        compiler_params=pltpu.CompilerParams(
            collective_id=0, has_side_effects=True, vmem_limit_bytes=56 * 2**20
        ),
        cost_estimate=pl.CostEstimate(
            flops=18 * rows * sites * sites, bytes_accessed=8 * rows * sites, transcendentals=0
        ),
    )(coupling, field)


def solution(mesh):
    return jax.shard_map(
        functools.partial(per_device, mesh.shape["tm"], mesh.shape["rows"]),
        mesh=mesh,
        in_specs=(P("tm", "rows", None), P("tm", "rows")),
        out_specs=P("tm", "rows", None),
        check_vma=False,
    )
```

time: 214 us -> 136 us (0.64)
  the two profiles are of different devices: /device:TPU:1 before, /device:TPU:48 now
where the time goes in v1:
time: 136 us
  Pallas kernels  133 us (98%)
  local copies, waits for them, and re-layouts  2.31 us (2%)
    pallas_call x1, Pallas kernels, per_device(): pl.pallas_call(functools.partial(kernel, n_t, n_r), out_shape=jax.ShapeDt...  133 us

profile of v1, /device:TPU:48, one launch (start us, length us, event | category | flops | bytes accessed | tf_op | source)
XLA Modules:
  0.0 135.8 jit_solution(18184569278130194299)
XLA Ops:
  0.0 133.5 %shard_map.28 = f32[1,256,1024]{2,1,0:T(8,128)} custom-call(f32[1,256,1024]{2,1,0:T(8,128)} %coupling.1, f32[1,256]{1,0:T(1,128)} %field.1), custom_call_target="tpu_custom_call" | custom-call | flops 4831838208 | bytes 2097152 | tf_op jit(solution)/shard_map/pallas_call | solution.py:314
  133.5 2.3 %copy.4 = f32[1,256,1024]{2,1,0:T(8,128)} copy(f32[1,256,1024]{2,1,0:T(8,128)} %shard_map.28) | data formatting | bytes 2097152

commit v2 on v1

--- a/solution.py
+++ b/solution.py
@@ -13,7 +13,7 @@
 
 WIDE = 128
 AHEAD = 2
-START = 6
+START = 5
 
 
 def split(x):
@@ -31,8 +31,8 @@
 def kernel(
     n_t, n_r, coupling, field, out,
     raw, full, sib, rowbuf, lhs_h, lhs_l, own_h, own_l, one_h, one_l,
-    stage_a, stage_b, land_a, land_b, acc, res,
-    local_sem, out_sem,
+    stage_a, stage_b, land_a, land_b, acc, res, meet_h, meet_l,
+    rel, local_sem, out_sem, rel_s, rel_r,
     own_s, own_r, fwd_s, fwd_r, sib_s, sib_r, xo_s, xo_r, row_s, row_r, a_s, a_r, b_s, b_r,
 ):
     t = lax.axis_index("tm")
@@ -41,6 +41,24 @@
     nch = full.shape[0]
     even = lax.rem(t, 2) == 0
     half = rows // 2
+    span = n_t // 2
+    place = lax.rem(t, span)
+    base = t - place
+    other = span - base
+    line = 16
+    n_rel = nch - 1
+    odd = jnp.logical_not(even)
+    is_src = place == 0
+    is_dst = place >= span - 2
+    kind = place // line - 1
+    mine = lax.rem(place, line) // 2
+    is_rel = jnp.logical_and(
+        jnp.logical_and(kind >= 0, mine < n_rel),
+        jnp.logical_or(jnp.logical_and(even, kind == 0), jnp.logical_and(odd, kind > 0)),
+    )
+
+    def way(k, c):
+        return (k + 1) * line + 2 * c + (1 if k else 0)
 
     def tm(by):
         return lax.rem(t + by + n_t, n_t)
@@ -54,8 +72,16 @@
     def plane(by):
         return pl.multiple_of(lax.rem(r + by + n_r, n_r) * rows, rows)
 
-    load = pltpu.make_async_copy(coupling.at[0], raw, local_sem)
-    load.start()
+    def load(c):
+        return pltpu.make_async_copy(
+            coupling.at[0, :, cols(c)], raw.at[:, cols(c)], local_sem.at[c]
+        )
+
+    def cols(c):
+        return pl.ds(pl.multiple_of(c * WIDE, WIDE), WIDE)
+
+    for c in range(nch):
+        load(c).start()
 
     barrier = pltpu.get_barrier_semaphore()
     for by in (1, -1):
@@ -65,6 +91,25 @@
     @pl.when(even)
     def _():
         pl.semaphore_signal(barrier, inc=1, device_id=at_t(2), device_id_type=MESH)
+
+    @pl.when(is_rel)
+    def _():
+        for to in (base, other + place):
+            pl.semaphore_signal(barrier, inc=1, device_id=(to, r), device_id_type=MESH)
+
+    def greet(k):
+        for c in range(n_rel):
+            to = (base + way(k, c), r)
+            pl.semaphore_signal(barrier, inc=1, device_id=to, device_id_type=MESH)
+
+    @pl.when(jnp.logical_and(is_dst, even))
+    def _():
+        greet(1)
+
+    @pl.when(jnp.logical_and(is_dst, odd))
+    def _():
+        greet(0)
+        greet(2)
 
     def copy(src, dst, ssem, rsem, dev):
         return pltpu.make_async_remote_copy(
@@ -94,8 +139,9 @@
     def xo(c):
         return copy(stage_a.at[c], land_a.at[c], xo_s.at[c], xo_r.at[c], at_t(-1))
 
-    def row():
-        return copy(full.at[:, pl.ds(plane(0), rows), :], rowbuf, row_s, row_r, at_t(-1))
+    def row(c):
+        piece = full.at[c, pl.ds(plane(0), rows), :]
+        return copy(piece, rowbuf.at[c], row_s.at[c], row_r.at[c], at_t(-1))
 
     def send_a(c):
         return copy(stage_a.at[c], land_b.at[c], a_s.at[c], a_r.at[c], at_t(-2))
@@ -103,25 +149,83 @@
     def send_b(c):
         return copy(stage_b.at[c], land_b.at[c], b_s.at[c], b_r.at[c], at_t(-1))
 
-    def cols(c):
-        return pl.ds(pl.multiple_of(c * WIDE, WIDE), WIDE)
+    def by_way(k, c):
+        src = (full.at[c, pl.ds(plane(0), rows), :], stage_a.at[c], stage_b.at[c])[k]
+        sem = (row_s, a_s, b_s)[k].at[c]
+        return copy(src, rel.at[0], sem, rel_r.at[0], (base + way(k, c), r))
+
+    def start(k, c):
+        go = (row, send_a, send_b)[k]
+        by = jnp.logical_and(is_src, c < n_rel)
+
+        @pl.when(by)
+        def _():
+            by_way(k, c).start()
+
+        @pl.when(jnp.logical_not(by))
+        def _():
+            go(c).start()
+
+    def over():
+        return copy(rel.at[0], rel.at[1], rel_s.at[0], rel_r.at[1], (other + place, r))
+
+    def last_leg(k):
+        dst, sem, back = ((rowbuf, row_r, 1), (land_b, a_r, 2), (land_b, b_r, 1))[k]
+        to = (lax.rem(other - back + n_t, n_t), r)
+        return copy(rel.at[1], dst.at[mine], rel_s.at[1], sem.at[mine], to)
+
+    def hand_on(kinds):
+        @pl.when(is_rel)
+        def _():
+            copy(rel.at[0], rel.at[0], rel_s.at[0], rel_r.at[0], (base, r)).wait_recv()
+            over().start()
+            over().wait_recv()
+
+        for k in kinds:
+
+            @pl.when(jnp.logical_and(is_rel, kind == k))
+            def _():
+                last_leg(k).start()
+
+    def handed(kinds):
+        for k in kinds:
+
+            @pl.when(jnp.logical_and(is_rel, kind == k))
+            def _():
+                over().wait_send()
+                last_leg(k).wait_send()
 
     scale = jnp.exp(jnp.transpose(jnp.broadcast_to(field[...], (WIDE, rows))))
-    load.wait()
     row_ids = lax.broadcasted_iota(jnp.int32, (rows, WIDE), 0) + r * rows
     col_ids = lax.broadcasted_iota(jnp.int32, (rows, WIDE), 1)
 
     def build(c, _):
+        load(c).wait()
         ident = jnp.where(row_ids == col_ids + c * WIDE, 1.0, 0.0).astype(F32)
         full[c, pl.ds(plane(0), rows), :] = scale * (ident + raw[:, cols(c)])
         return 0
 
-    lax.fori_loop(0, nch, build, 0)
-
-    def gather(process):
+    lax.fori_loop(0, AHEAD, build, 0)
+
+    def rest_of_block():
+        lax.fori_loop(AHEAD, nch, build, 0)
+
+        def send(c, _):
+            start(0, c)
+
+            @pl.when(is_src)
+            def _():
+                row(c).wait_send()
+
+            return 0
+
+        lax.fori_loop(0, nch, send, 0)
+
+    def gather(process, before):
         for c in range(AHEAD):
             for d in (0, 1):
                 own(c, d).start()
+        before()
 
         def step(c, _):
             @pl.when(c < nch)
@@ -162,25 +266,24 @@
 
     @pl.when(jnp.logical_not(even))
     def _():
-        pl.semaphore_wait(barrier, 3)
-        row().start()
+        pl.semaphore_wait(barrier, jnp.where(is_rel, 5, 3))
 
         def left_factor():
-            row().wait_recv()
-
             def body(c, _):
+                row(c).wait_recv()
                 fill_lhs(c, 0)
                 return 0
 
             lax.fori_loop(0, nch, body, 0)
 
-        def product(c):
+        def product(c, _):
             stage_a[c] = dot3(
                 lhs_h[0:rows, :], lhs_l[0:rows, :], one_h[:, cols(c)], one_l[:, cols(c)]
             )
             xo(c).start()
-
-        lag = 3
+            return 0
+
+        lag = 5
 
         def process(c):
             to_sib(c).start()
@@ -191,22 +294,20 @@
             @pl.when(c == lag)
             def _():
                 left_factor()
+                lax.fori_loop(0, lag, product, 0)
 
             @pl.when(c >= lag)
             def _():
-                product(c - lag)
-
-        gather(process)
-
-        def rest(c, _):
-            product(c)
-            return 0
-
-        lax.fori_loop(nch - lag, nch, rest, 0)
-
+                product(c, 0)
+
+        gather(process, rest_of_block)
         acc[...] = jnp.zeros_like(acc)
 
         def body(c, _):
+            @pl.when(c == mine)
+            def _():
+                hand_on((1, 2))
+
             send_b(c).wait_recv()
             add_chunk(c, land_b, acc)
             return 0
@@ -214,24 +315,28 @@
         lax.fori_loop(0, nch, body, 0)
         write = pltpu.make_async_copy(acc, out.at[0], out_sem.at[0])
         write.start()
-        row().wait_send()
 
         def finish(c, _):
+            row(c).wait_send()
             to_sib(c).wait_send()
             xo(c).wait_send()
             return 0
 
         lax.fori_loop(0, nch, finish, 0)
         lax.fori_loop(0, nch, drain, 0)
+
+        handed((1, 2))
         write.wait()
 
     @pl.when(even)
     def _():
-        pl.semaphore_wait(barrier, 4)
-        row().start()
-        row().wait_recv()
+        pl.semaphore_wait(barrier, jnp.where(is_src, 4 + 3 * n_rel, jnp.where(is_rel, 6, 4)))
+        rest_of_block()
+
+        hand_on((0,))
 
         def fill(c, _):
+            row(c).wait_recv()
             fill_lhs(c, 0)
             return 0
 
@@ -245,9 +350,6 @@
             return 0
 
         lax.fori_loop(0, START, take, 0)
-        acc[...] = jnp.zeros_like(acc)
-        lag = 2
-
         def process(c):
             @pl.when(c == 0)
             def _():
@@ -267,41 +369,55 @@
             own_l[:, cols(c)] = bl
             y = dot3(lhs_h[...], lhs_l[...], bh, bl)
             stage_a[c] = y[0:rows]
-            send_a(c).start()
+            start(1, c)
             stage_b[c] = y[rows:]
-            send_b(c).start()
-
-            @pl.when(c >= lag)
-            def _():
-                send_a(c - lag).wait_recv()
-                add_chunk(c - lag, land_b, acc)
-
-        gather(process)
-
-        def rest(c, _):
+            start(2, c)
+
+        gather(process, lambda: None)
+
+        def collect(c, _):
             send_a(c).wait_recv()
-            add_chunk(c, land_b, acc)
-            return 0
-
-        lax.fori_loop(nch - lag, nch, rest, 0)
-
-        xh, xl = split(acc[...])
+            hi, lo = split(land_b[c])
+            lhs_h[0:rows, cols(c)] = hi
+            lhs_l[0:rows, cols(c)] = lo
+            return 0
+
+        lax.fori_loop(0, nch - 1, collect, 0)
+
+        cut = (nch - 1) * WIDE
         wide = 2 * WIDE
-        for k in range(nch // 2):
-            part = slice(k * wide, (k + 1) * wide)
-            res[k] = dot3(xh, xl, own_h[:, part], own_l[:, part])
+        parts = [slice(k * wide, (k + 1) * wide) for k in range(nch // 2)]
+        fh, fl = lhs_h[0:rows, 0:cut], lhs_l[0:rows, 0:cut]
+        for part in parts:
+            x = dot3(fh, fl, one_h[0:cut, part], one_l[0:cut, part])
+            lhs_h[rows:, part], lhs_l[rows:, part] = split(x)
+        xh, xl = lhs_h[rows:, :], lhs_l[rows:, :]
+        gh, gl = one_h[cut:, :], one_l[cut:, :]
+        for k, part in enumerate(parts):
+            vh, vl = own_h[:, part], own_l[:, part]
+            res[k] = dot3(xh, xl, vh, vl)
+            meet_h[:, part], meet_l[:, part] = split(dot3(gh, gl, vh, vl))
+
+        send_a(nch - 1).wait_recv()
+        lh, ll = split(land_b[nch - 1])
+        for k, part in enumerate(parts):
+            res[k] += dot3(lh, ll, meet_h[:, part], meet_l[:, part])
             pltpu.make_async_copy(res.at[k], out.at[0, :, part], out_sem.at[k]).start()
-        row().wait_send()
 
         def finish(c, _):
+            @pl.when(jnp.logical_not(is_src))
+            def _():
+                row(c).wait_send()
+
             send_a(c).wait_send()
             send_b(c).wait_send()
             return 0
 
         lax.fori_loop(0, nch, finish, 0)
         lax.fori_loop(0, nch, drain, 0)
-        for k in range(nch // 2):
-            part = slice(k * wide, (k + 1) * wide)
+
+        handed((0,))
+        for k, part in enumerate(parts):
             pltpu.make_async_copy(res.at[k], out.at[0, :, part], out_sem.at[k]).wait()
 
 
@@ -336,8 +452,13 @@
             piece,
             pltpu.VMEM((rows, sites), F32),
             pltpu.VMEM((nch // 2, rows, 2 * WIDE), F32),
-            dma,
-            dma((nch,)),
+            pltpu.VMEM((WIDE, sites), BF16),
+            pltpu.VMEM((WIDE, sites), BF16),
+            pltpu.VMEM((2, rows, WIDE), F32),
+            dma((nch,)),
+            dma((nch,)),
+            dma((2,)),
+            dma((2,)),
             dma((2, nch)),
             dma((2, nch)),
             dma((2, nch)),
@@ -346,8 +467,8 @@
             dma((nch,)),
             dma((nch,)),
             dma((nch,)),
-            dma,
-            dma,
+            dma((nch,)),
+            dma((nch,)),
             dma((nch,)),
             dma((nch,)),
             dma((nch,)),

time: 136 us -> 102 us (0.75)
  the two profiles are of different devices: /device:TPU:48 before, /device:TPU:62 now
where the time goes in v2:
time: 102 us
  Pallas kernels  99.5 us (98%)
  local copies, waits for them, and re-layouts  2.31 us (2%)
    pallas_call x1, Pallas kernels, per_device(): pl.pallas_call(functools.partial(kernel, n_t, n_r), out_shape=jax.ShapeDt...  99.5 us
    unnamed x1, local copies, waits for them, and re-layouts  2.31 us

profile of v2, /device:TPU:62, one launch (start us, length us, event | category | flops | bytes accessed | tf_op | source)
XLA Modules:
  0.0 101.8 jit_solution(3964744453583824433)
XLA Ops:
  0.0 99.5 %shard_map.28 = f32[1,256,1024]{2,1,0:T(8,128)} custom-call(f32[1,256,1024]{2,1,0:T(8,128)} %coupling.1, f32[1,256]{1,0:T(1,128)} %field.1), custom_call_target="tpu_custom_call" | custom-call | flops 4831838208 | bytes 2097152 | tf_op jit(solution)/shard_map/pallas_call | solution.py:430
  99.5 2.3 %copy.4 = f32[1,256,1024]{2,1,0:T(8,128)} copy(f32[1,256,1024]{2,1,0:T(8,128)} %shard_map.28) | data formatting | bytes 2097152

commit v3 on v2

--- a/solution.py
+++ b/solution.py
@@ -13,6 +13,8 @@
 
 WIDE = 128
 AHEAD = 2
+FOLD = 2
+LEAD = 1
 START = 5
 
 
@@ -30,14 +32,14 @@
 
 def kernel(
     n_t, n_r, coupling, field, out,
-    raw, full, sib, rowbuf, lhs_h, lhs_l, own_h, own_l, one_h, one_l,
-    stage_a, stage_b, land_a, land_b, acc, res, meet_h, meet_l,
-    rel, local_sem, out_sem, rel_s, rel_r,
+    full, sib, rowbuf, lhs_h, lhs_l, own_h, own_l, one_h, one_l,
+    stage_a, stage_b, land_a, land_b, meet_h, meet_l,
+    rel, pace, rel_s, rel_r,
     own_s, own_r, fwd_s, fwd_r, sib_s, sib_r, xo_s, xo_r, row_s, row_r, a_s, a_r, b_s, b_r,
 ):
     t = lax.axis_index("tm")
     r = lax.axis_index("rows")
-    rows = raw.shape[0]
+    rows = coupling.shape[1]
     nch = full.shape[0]
     even = lax.rem(t, 2) == 0
     half = rows // 2
@@ -46,15 +48,15 @@
     base = t - place
     other = span - base
     line = 16
-    n_rel = nch - 1
+    n_rel = (nch, nch - 1, nch - 1)
     odd = jnp.logical_not(even)
     is_src = place == 0
     is_dst = place >= span - 2
     kind = place // line - 1
     mine = lax.rem(place, line) // 2
-    is_rel = jnp.logical_and(
-        jnp.logical_and(kind >= 0, mine < n_rel),
-        jnp.logical_or(jnp.logical_and(even, kind == 0), jnp.logical_and(odd, kind > 0)),
+    is_rel = jnp.logical_or(
+        jnp.logical_and(even, kind == 0),
+        jnp.logical_and(odd, jnp.logical_and(kind > 0, mine < n_rel[1])),
     )
 
     def way(k, c):
@@ -72,16 +74,8 @@
     def plane(by):
         return pl.multiple_of(lax.rem(r + by + n_r, n_r) * rows, rows)
 
-    def load(c):
-        return pltpu.make_async_copy(
-            coupling.at[0, :, cols(c)], raw.at[:, cols(c)], local_sem.at[c]
-        )
-
     def cols(c):
         return pl.ds(pl.multiple_of(c * WIDE, WIDE), WIDE)
-
-    for c in range(nch):
-        load(c).start()
 
     barrier = pltpu.get_barrier_semaphore()
     for by in (1, -1):
@@ -97,8 +91,11 @@
         for to in (base, other + place):
             pl.semaphore_signal(barrier, inc=1, device_id=(to, r), device_id_type=MESH)
 
+    beside = (other + place, r)
+    pl.semaphore_signal(barrier, inc=1, device_id=beside, device_id_type=MESH)
+
     def greet(k):
-        for c in range(n_rel):
+        for c in range(n_rel[k]):
             to = (base + way(k, c), r)
             pl.semaphore_signal(barrier, inc=1, device_id=to, device_id_type=MESH)
 
@@ -156,7 +153,7 @@
 
     def start(k, c):
         go = (row, send_a, send_b)[k]
-        by = jnp.logical_and(is_src, c < n_rel)
+        by = jnp.logical_and(is_src, c < n_rel[k])
 
         @pl.when(by)
         def _():
@@ -200,9 +197,8 @@
     col_ids = lax.broadcasted_iota(jnp.int32, (rows, WIDE), 1)
 
     def build(c, _):
-        load(c).wait()
         ident = jnp.where(row_ids == col_ids + c * WIDE, 1.0, 0.0).astype(F32)
-        full[c, pl.ds(plane(0), rows), :] = scale * (ident + raw[:, cols(c)])
+        full[c, pl.ds(plane(0), rows), :] = scale * (ident + coupling[0, :, cols(c)])
         return 0
 
     lax.fori_loop(0, AHEAD, build, 0)
@@ -234,8 +230,16 @@
                     own_in(c, d).wait_recv()
                     fwd(c, d).start()
 
+            @pl.when(c + AHEAD + LEAD < nch)
+            def _():
+                pl.semaphore_signal(pace, inc=1, device_id=beside, device_id_type=MESH)
+
             @pl.when(c + AHEAD < nch)
             def _():
+                @pl.when(c >= LEAD)
+                def _():
+                    pl.semaphore_wait(pace, 1)
+
                 for d in (0, 1):
                     own(c + AHEAD, d).start()
 
@@ -260,13 +264,13 @@
         lhs_h[first : first + rows, cols(c)] = hi
         lhs_l[first : first + rows, cols(c)] = lo
 
-    def add_chunk(c, land, total):
-        h, l = split(land[c])
-        total[...] += dot3(h, l, one_h[cols(c), :], one_l[cols(c), :])
+    def add_chunk(c):
+        h, l = split(land_b[c])
+        out[0] += dot3(h, l, one_h[cols(c), :], one_l[cols(c), :])
 
     @pl.when(jnp.logical_not(even))
     def _():
-        pl.semaphore_wait(barrier, jnp.where(is_rel, 5, 3))
+        pl.semaphore_wait(barrier, jnp.where(is_rel, 6, 4))
 
         def left_factor():
             def body(c, _):
@@ -301,7 +305,7 @@
                 product(c, 0)
 
         gather(process, rest_of_block)
-        acc[...] = jnp.zeros_like(acc)
+        out[...] = jnp.zeros_like(out)
 
         def body(c, _):
             @pl.when(c == mine)
@@ -309,12 +313,10 @@
                 hand_on((1, 2))
 
             send_b(c).wait_recv()
-            add_chunk(c, land_b, acc)
+            add_chunk(c)
             return 0
 
         lax.fori_loop(0, nch, body, 0)
-        write = pltpu.make_async_copy(acc, out.at[0], out_sem.at[0])
-        write.start()
 
         def finish(c, _):
             row(c).wait_send()
@@ -326,11 +328,9 @@
         lax.fori_loop(0, nch, drain, 0)
 
         handed((1, 2))
-        write.wait()
-
     @pl.when(even)
     def _():
-        pl.semaphore_wait(barrier, jnp.where(is_src, 4 + 3 * n_rel, jnp.where(is_rel, 6, 4)))
+        pl.semaphore_wait(barrier, jnp.where(is_src, 5 + sum(n_rel), jnp.where(is_rel, 7, 5)))
         rest_of_block()
 
         hand_on((0,))
@@ -367,10 +367,9 @@
             bh, bl = split(full[c])
             own_h[:, cols(c)] = bh
             own_l[:, cols(c)] = bl
-            y = dot3(lhs_h[...], lhs_l[...], bh, bl)
-            stage_a[c] = y[0:rows]
+            stage_a[c] = dot3(lhs_h[0:rows, :], lhs_l[0:rows, :], bh, bl)
             start(1, c)
-            stage_b[c] = y[rows:]
+            stage_b[c] = dot3(lhs_h[rows:, :], lhs_l[rows:, :], bh, bl)
             start(2, c)
 
         gather(process, lambda: None)
@@ -382,9 +381,9 @@
             lhs_l[0:rows, cols(c)] = lo
             return 0
 
-        lax.fori_loop(0, nch - 1, collect, 0)
-
-        cut = (nch - 1) * WIDE
+        lax.fori_loop(0, nch - FOLD, collect, 0)
+
+        cut = (nch - FOLD) * WIDE
         wide = 2 * WIDE
         parts = [slice(k * wide, (k + 1) * wide) for k in range(nch // 2)]
         fh, fl = lhs_h[0:rows, 0:cut], lhs_l[0:rows, 0:cut]
@@ -393,16 +392,15 @@
             lhs_h[rows:, part], lhs_l[rows:, part] = split(x)
         xh, xl = lhs_h[rows:, :], lhs_l[rows:, :]
         gh, gl = one_h[cut:, :], one_l[cut:, :]
-        for k, part in enumerate(parts):
+        for part in parts:
             vh, vl = own_h[:, part], own_l[:, part]
-            res[k] = dot3(xh, xl, vh, vl)
+            out[0, :, part] = dot3(xh, xl, vh, vl)
             meet_h[:, part], meet_l[:, part] = split(dot3(gh, gl, vh, vl))
 
-        send_a(nch - 1).wait_recv()
-        lh, ll = split(land_b[nch - 1])
-        for k, part in enumerate(parts):
-            res[k] += dot3(lh, ll, meet_h[:, part], meet_l[:, part])
-            pltpu.make_async_copy(res.at[k], out.at[0, :, part], out_sem.at[k]).start()
+        lax.fori_loop(nch - FOLD, nch, collect, 0)
+        lh, ll = lhs_h[0:rows, cut:], lhs_l[0:rows, cut:]
+        for part in parts:
+            out[0, :, part] += dot3(lh, ll, meet_h[:, part], meet_l[:, part])
 
         def finish(c, _):
             @pl.when(jnp.logical_not(is_src))
@@ -417,8 +415,6 @@
         lax.fori_loop(0, nch, drain, 0)
 
         handed((0,))
-        for k, part in enumerate(parts):
-            pltpu.make_async_copy(res.at[k], out.at[0, :, part], out_sem.at[k]).wait()
 
 
 def per_device(n_t, n_r, coupling, field):
@@ -427,16 +423,15 @@
     dma = pltpu.SemaphoreType.DMA
     piece = pltpu.VMEM((nch, rows, WIDE), F32)
     whole = pltpu.VMEM((nch, sites, WIDE), F32)
-    return pl.pallas_call(
+    done = pl.pallas_call(
         functools.partial(kernel, n_t, n_r),
         out_shape=jax.ShapeDtypeStruct((1, rows, sites), F32),
         in_specs=[
-            pl.BlockSpec(memory_space=pl.ANY),
+            pl.BlockSpec(memory_space=pltpu.VMEM),
             pl.BlockSpec(memory_space=pltpu.VMEM),
         ],
-        out_specs=pl.BlockSpec(memory_space=pl.ANY),
+        out_specs=pl.BlockSpec(memory_space=pltpu.VMEM),
         scratch_shapes=[
-            pltpu.VMEM((rows, sites), F32),
             whole,
             whole,
             piece,
@@ -450,13 +445,10 @@
             piece,
             piece,
             piece,
-            pltpu.VMEM((rows, sites), F32),
-            pltpu.VMEM((nch // 2, rows, 2 * WIDE), F32),
-            pltpu.VMEM((WIDE, sites), BF16),
-            pltpu.VMEM((WIDE, sites), BF16),
+            pltpu.VMEM((FOLD * WIDE, sites), BF16),
+            pltpu.VMEM((FOLD * WIDE, sites), BF16),
             pltpu.VMEM((2, rows, WIDE), F32),
-            dma((nch,)),
-            dma((nch,)),
+            pltpu.SemaphoreType.REGULAR,
             dma((2,)),
             dma((2,)),
             dma((2, nch)),
@@ -475,12 +467,35 @@
             dma((nch,)),
         ],
         compiler_params=pltpu.CompilerParams(
-            collective_id=0, has_side_effects=True, vmem_limit_bytes=56 * 2**20
+            collective_id=0, has_side_effects=True, vmem_limit_bytes=40 * 2**20
         ),
         cost_estimate=pl.CostEstimate(
             flops=18 * rows * sites * sites, bytes_accessed=8 * rows * sites, transcendentals=0
         ),
     )(coupling, field)
+    pieces = 4
+
+    def write(src, dst, sems):
+        step = rows // pieces
+        copies = [
+            pltpu.make_async_copy(
+                src.at[0, pl.ds(i * step, step)], dst.at[0, pl.ds(i * step, step)], sems.at[i]
+            )
+            for i in range(pieces)
+        ]
+        for c in copies:
+            c.start()
+        for c in copies:
+            c.wait()
+
+    return pl.pallas_call(
+        write,
+        out_shape=jax.ShapeDtypeStruct((1, rows, sites), F32),
+        in_specs=[pl.BlockSpec(memory_space=pl.ANY)],
+        out_specs=pl.BlockSpec(memory_space=pl.ANY),
+        scratch_shapes=[dma((pieces,))],
+        compiler_params=pltpu.CompilerParams(vmem_limit_bytes=2**20),
+    )(done)
 
 
 def solution(mesh):

time: 102 us -> 101 us (level)
    pallas_call x1, Pallas kernels: 99.5 us -> 98.3 us  [per_device(): pl.pallas_call(functools.partial(kernel, n_t, n_r), out_shape=jax.ShapeDt...]
    unnamed x1 -> x4, local copies, waits for them, and re-layouts: 2.31 us -> 1.9 us
where the time goes in v3:
time: 101 us
  Pallas kernels  99.3 us (98%)
  local copies, waits for them, and re-layouts  1.9 us (2%)
    pallas_call x1, Pallas kernels, per_device(): pl.pallas_call(functools.partial(kernel, n_t, n_r), out_shape=jax.ShapeDt...  98.3 us

profile of v3, /device:TPU:62, one launch (start us, length us, event | category | flops | bytes accessed | tf_op | source)
XLA Modules:
  0.0 101.2 jit_solution(7597310841128912983)
XLA Ops:
  0.0 0.0 copy-start
  0.0 1.2 %copy-done = f32[1,256,1024]{2,1,0:T(8,128)S(1)} copy-done((f32[1,256,1024]{2,1,0:T(8,128)S(1)}, f32[1,256,1024]{2,1,0:T(8,128)}, u32[]{:S(2)}) %copy-start) | copy-done | bytes 1048600
  1.2 0.0 copy-start.1
  1.2 0.7 copy-done.1
  1.9 98.3 %shard_map.28.src = f32[1,256,1024]{2,1,0:T(8,128)S(1)} custom-call(f32[1,256,1024]{2,1,0:T(8,128)S(1)} %copy-done, f32[1,256]{1,0:T(1,128)S(1)} %copy-done.1), custom_call_target="tpu_custom_call" | custom-call | flops 4831838208 | bytes 2097152 | tf_op jit(solution)/shard_map/pallas_call | solution.py:426
  100.2 1.0 shard_map.29
Async XLA Ops:
  0.0 1.2 %copy-start = (f32[1,256,1024]{2,1,0:T(8,128)S(1)}, f32[1,256,1024]{2,1,0:T(8,128)}, u32[]{:S(2)}) copy-start(f32[1,256,1024]{2,1,0:T(8,128)} %coupling.1) | copy-start | bytes 3145732
  1.2 0.7 copy-start.1

commit v4 on v3

--- a/solution.py
+++ b/solution.py
@@ -32,9 +32,9 @@
 
 def kernel(
     n_t, n_r, coupling, field, out,
-    full, sib, rowbuf, lhs_h, lhs_l, own_h, own_l, one_h, one_l,
+    raw, levels, full, sib, rowbuf, lhs_h, lhs_l, own_h, own_l, one_h, one_l,
     stage_a, stage_b, land_a, land_b, meet_h, meet_l,
-    rel, pace, rel_s, rel_r,
+    rel, load_sem, pace, rel_s, rel_r,
     own_s, own_r, fwd_s, fwd_r, sib_s, sib_r, xo_s, xo_r, row_s, row_r, a_s, a_r, b_s, b_r,
 ):
     t = lax.axis_index("tm")
@@ -77,6 +77,15 @@
     def cols(c):
         return pl.ds(pl.multiple_of(c * WIDE, WIDE), WIDE)
 
+    def load(c):
+        src = coupling.at[0, :, cols(c)]
+        return pltpu.make_async_copy(src, raw.at[:, cols(c)], load_sem.at[c])
+
+    load_levels = pltpu.make_async_copy(field, levels, load_sem.at[nch])
+    load_levels.start()
+    for c in range(nch):
+        load(c).start()
+
     barrier = pltpu.get_barrier_semaphore()
     for by in (1, -1):
         pl.semaphore_signal(barrier, inc=1, device_id=at_r(by), device_id_type=MESH)
@@ -192,13 +201,15 @@
                 over().wait_send()
                 last_leg(k).wait_send()
 
-    scale = jnp.exp(jnp.transpose(jnp.broadcast_to(field[...], (WIDE, rows))))
+    load_levels.wait()
+    scale = jnp.exp(jnp.transpose(jnp.broadcast_to(levels[...], (WIDE, rows))))
     row_ids = lax.broadcasted_iota(jnp.int32, (rows, WIDE), 0) + r * rows
     col_ids = lax.broadcasted_iota(jnp.int32, (rows, WIDE), 1)
 
     def build(c, _):
+        load(c).wait()
         ident = jnp.where(row_ids == col_ids + c * WIDE, 1.0, 0.0).astype(F32)
-        full[c, pl.ds(plane(0), rows), :] = scale * (ident + coupling[0, :, cols(c)])
+        full[c, pl.ds(plane(0), rows), :] = scale * (ident + raw[:, cols(c)])
         return 0
 
     lax.fori_loop(0, AHEAD, build, 0)
@@ -427,11 +438,13 @@
         functools.partial(kernel, n_t, n_r),
         out_shape=jax.ShapeDtypeStruct((1, rows, sites), F32),
         in_specs=[
-            pl.BlockSpec(memory_space=pltpu.VMEM),
-            pl.BlockSpec(memory_space=pltpu.VMEM),
+            pl.BlockSpec(memory_space=pltpu.HBM),
+            pl.BlockSpec(memory_space=pltpu.HBM),
         ],
         out_specs=pl.BlockSpec(memory_space=pltpu.VMEM),
         scratch_shapes=[
+            pltpu.VMEM((rows, sites), F32),
+            pltpu.VMEM((1, rows), F32),
             whole,
             whole,
             piece,
@@ -448,6 +461,7 @@
             pltpu.VMEM((FOLD * WIDE, sites), BF16),
             pltpu.VMEM((FOLD * WIDE, sites), BF16),
             pltpu.VMEM((2, rows, WIDE), F32),
+            dma((nch + 1,)),
             pltpu.SemaphoreType.REGULAR,
             dma((2,)),
             dma((2,)),
@@ -467,7 +481,7 @@
             dma((nch,)),
         ],
         compiler_params=pltpu.CompilerParams(
-            collective_id=0, has_side_effects=True, vmem_limit_bytes=40 * 2**20
+            collective_id=0, has_side_effects=True, vmem_limit_bytes=52 * 2**20
         ),
         cost_estimate=pl.CostEstimate(
             flops=18 * rows * sites * sites, bytes_accessed=8 * rows * sites, transcendentals=0

time: 101 us -> 99.5 us (0.985)
  local copies, waits for them, and re-layouts: 1.9 us -> 0.68 us
    unnamed x4 -> x2, local copies, waits for them, and re-layouts: 1.9 us -> 0.68 us
where the time goes in v4:
time: 99.5 us; the launch traced here: 99.3 us
  Pallas kernels  98.7 us (99%)
    pallas_call x1, Pallas kernels, per_device(): pl.pallas_call(functools.partial(kernel, n_t, n_r), out_shape=jax.ShapeDt...  97.7 us

profile of v4, /device:TPU:62, one launch (start us, length us, event | category | flops | bytes accessed | tf_op | source)
XLA Modules:
  0.0 99.3 jit_solution(4384067850306926346)
XLA Ops:
  0.0 0.0 copy-start
  0.0 0.7 copy-done
  0.7 97.7 %shard_map.28.src = f32[1,256,1024]{2,1,0:T(8,128)S(1)} custom-call(f32[1,256,1024]{2,1,0:T(8,128)} %coupling.1, f32[1,256]{1,0:T(1,128)S(1)} %copy-done), custom_call_target="tpu_custom_call" | custom-call | flops 4831838208 | bytes 2097152 | tf_op jit(solution)/shard_map/pallas_call | solution.py:437
  98.3 1.0 %shard_map.29 = f32[1,256,1024]{2,1,0:T(8,128)} custom-call(f32[1,256,1024]{2,1,0:T(8,128)S(1)} %shard_map.28.src), custom_call_target="tpu_custom_call" | custom-call | tf_op jit(solution)/shard_map/pallas_call | solution.py:505
Async XLA Ops:
  0.0 0.7 copy-start

commit v5 on v4

--- a/solution.py
+++ b/solution.py
@@ -15,6 +15,7 @@
 AHEAD = 2
 FOLD = 2
 LEAD = 1
+HOLD = 1
 START = 5
 
 
@@ -228,7 +229,7 @@
 
         lax.fori_loop(0, nch, send, 0)
 
-    def gather(process, before):
+    def gather(process, before, done):
         for c in range(AHEAD):
             for d in (0, 1):
                 own(c, d).start()
@@ -254,12 +255,13 @@
                 for d in (0, 1):
                     own(c + AHEAD, d).start()
 
-            @pl.when(c >= 1)
-            def _():
+            def take_in(k, _):
                 for d in (0, 1):
-                    fwd_in(c - 1, d).wait_recv()
-                process(c - 1)
-
+                    fwd_in(k, d).wait_recv()
+                process(k)
+                return 0
+
+            lax.fori_loop(done(c - 1), done(c), take_in, 0)
             return 0
 
         lax.fori_loop(0, nch + 1, step, 0)
@@ -315,7 +317,7 @@
             def _():
                 product(c, 0)
 
-        gather(process, rest_of_block)
+        gather(process, rest_of_block, lambda c: jnp.maximum(c, 0))
         out[...] = jnp.zeros_like(out)
 
         def body(c, _):
@@ -376,14 +378,17 @@
                 lax.fori_loop(0, nch, body, 0)
 
             bh, bl = split(full[c])
-            own_h[:, cols(c)] = bh
-            own_l[:, cols(c)] = bl
             stage_a[c] = dot3(lhs_h[0:rows, :], lhs_l[0:rows, :], bh, bl)
             start(1, c)
             stage_b[c] = dot3(lhs_h[rows:, :], lhs_l[rows:, :], bh, bl)
             start(2, c)
-
-        gather(process, lambda: None)
+            own_h[:, cols(c)] = bh
+            own_l[:, cols(c)] = bl
+
+        def done(c):
+            return jnp.maximum(jnp.minimum(2 * (c - HOLD), c), 0)
+
+        gather(process, lambda: None, done)
 
         def collect(c, _):
             send_a(c).wait_recv()

time: 99.5 us -> 99.8 us (level)
  no operation moved by 1% of the time
where the time goes in v5:
time: 99.8 us; the launch traced here: 99.7 us
  Pallas kernels  99 us (99%)
    pallas_call x1, Pallas kernels, per_device(): pl.pallas_call(functools.partial(kernel, n_t, n_r), out_shape=jax.ShapeDt...  98 us

profile of v5, /device:TPU:62, one launch (start us, length us, event | category | flops | bytes accessed | tf_op | source)
XLA Modules:
  0.0 99.7 jit_solution(5360884157836181270)
XLA Ops:
  0.0 0.0 copy-start
  0.0 0.7 copy-done
  0.7 98.0 %shard_map.28.src = f32[1,256,1024]{2,1,0:T(8,128)S(1)} custom-call(f32[1,256,1024]{2,1,0:T(8,128)} %coupling.1, f32[1,256]{1,0:T(1,128)S(1)} %copy-done), custom_call_target="tpu_custom_call" | custom-call | flops 4831838208 | bytes 2097152 | tf_op jit(solution)/shard_map/pallas_call | solution.py:442
  98.7 1.0 %shard_map.29 = f32[1,256,1024]{2,1,0:T(8,128)} custom-call(f32[1,256,1024]{2,1,0:T(8,128)S(1)} %shard_map.28.src), custom_call_target="tpu_custom_call" | custom-call | tf_op jit(solution)/shard_map/pallas_call | solution.py:510
Async XLA Ops:
  0.0 0.7 copy-start

commit v6 on v4

--- a/solution.py
+++ b/solution.py
@@ -487,7 +487,7 @@
             flops=18 * rows * sites * sites, bytes_accessed=8 * rows * sites, transcendentals=0
         ),
     )(coupling, field)
-    pieces = 4
+    pieces = 8
 
     def write(src, dst, sems):
         step = rows // pieces

time: 99.5 us -> 99.5 us (level)
  no operation moved by 1% of the time
where the time goes in v6:
time: 99.5 us; the launch traced here: 99.4 us
  Pallas kernels  98.7 us (99%)
    pallas_call x1, Pallas kernels, per_device(): pl.pallas_call(functools.partial(kernel, n_t, n_r), out_shape=jax.ShapeDt...  97.7 us

profile of v6, /device:TPU:62, one launch (start us, length us, event | category | flops | bytes accessed | tf_op | source)
XLA Modules:
  0.0 99.4 jit_solution(14679869100696869679)
XLA Ops:
  0.0 0.0 copy-start
  0.0 0.7 copy-done
  0.7 97.7 %shard_map.28.src = f32[1,256,1024]{2,1,0:T(8,128)S(1)} custom-call(f32[1,256,1024]{2,1,0:T(8,128)} %coupling.1, f32[1,256]{1,0:T(1,128)S(1)} %copy-done), custom_call_target="tpu_custom_call" | custom-call | flops 4831838208 | bytes 2097152 | tf_op jit(solution)/shard_map/pallas_call | solution.py:437
  98.3 1.0 %shard_map.29 = f32[1,256,1024]{2,1,0:T(8,128)} custom-call(f32[1,256,1024]{2,1,0:T(8,128)S(1)} %shard_map.28.src), custom_call_target="tpu_custom_call" | custom-call | tf_op jit(solution)/shard_map/pallas_call | solution.py:505
Async XLA Ops:
  0.0 0.7 copy-start
